TPU v7x, 512 devices: a whole 4x4x16 slice. The times are simulated.
512 devices in a mesh: visit: 32 (over z, x_lo), patch: 16 (over x_hi, y, core).
Axes of the slice: x: 4 (x_hi: 2, x_lo: 2; x = x_hi * 2 + x_lo), y: 4, z: 16, core: 2. Of those that a mesh axis runs over, the one named last changes fastest.
Arguments:
- templates: float32 [32, 2, 256, 1024], P('visit', None, 'patch'), may hold values from -16 to 16, as said below
- owners: int32 [2], replicated, may hold values from 0 to 31, as said below
- science: float32 [2, 32, 256, 1024], P(None, 'visit', 'patch'), may hold values from -40 to 40
- sci_var: float32 [2, 32, 256, 1024], P(None, 'visit', 'patch'), may hold values from 0.03 to 0.3
- bad_pixels: int32 [2, 32, 256, 1024], P(None, 'visit', 'patch'), may hold values 0 or 1
Outputs:
- significance: float32 [2, 32, 256, 1024], P(None, 'visit', 'patch')
Inputs may be any that keep to these rules, and one draw needn't show every extreme that they name: `owners`: the steps' entries are distinct indices of stored tiles, one of them always 32 - 1. `templates`: variances (index 1) lie in 0.01 to 0.1.
All inputs are finite; a program needn't handle non-finite values. No bound on the sum of `bad_pixels` on one device may be relied on, other than what follows from the above.
Results may differ from a plain program's by a relative error of at most 0.0003.
Values sent between devices are 32-bit elements; how exact they have to be, the bound alone decides.
A program may use at most 64 MiB of HBM per device.

v0:
```python
import jax
import jax.numpy as jnp
import numpy as np
from jax import lax
from jax.sharding import PartitionSpec as P

NPROF = 5
RAD = 10
STEPS = 2
ridge = 1.0


def from_root(block, axis, holder):
    block = jnp.where(lax.axis_index(axis) == holder, block, jnp.zeros_like(block))
    return lax.psum(block, axis)


def padded(cells, sides, width):
    for axis, dim in sides:
        count = lax.axis_size(axis)
        ends = count - 1
        head = lax.slice_in_dim(cells, 0, width, axis=dim)
        tail = lax.slice_in_dim(cells, cells.shape[dim] - width, cells.shape[dim], axis=dim)
        cells = jnp.concatenate(
            [
                lax.ppermute(tail, axis, [(i, (i + 1) % count) for i in range(ends)]),
                cells,
                lax.ppermute(head, axis, [((i + 1) % count, i) for i in range(ends)]),
            ],
            axis=dim,
        )
    return cells


def profile_table():
    offsets = np.arange(-RAD, RAD + 1) * 1.0
    recipe = [(1.0, 0), (1.5, 1), (2.0, 2), (3.0, 0), (4.0, 1)]
    profiles = []
    for spread, degree in recipe[:NPROF]:
        profile = offsets**degree * np.exp(-offsets * offsets / (2.0 * spread * spread))
        for earlier in profiles:
            profile = profile - np.dot(earlier, profile) * earlier
        profile = profile / np.sqrt(np.dot(profile, profile))
        profiles.append(profile)
    return np.stack(profiles)


def band_table(profiles, outputs, inputs):
    distance = jnp.arange(inputs)[None, :] - jnp.arange(outputs)[:, None]
    table = jnp.zeros((NPROF, outputs, inputs), jnp.float32)
    for offset in range(2 * RAD + 1):
        table = (
            table + profiles[:, offset, None, None] * (distance == offset).astype(jnp.float32)[None]
        )
    return table


def basis_images(extended):
    profiles = jnp.asarray(profile_table(), jnp.float32)
    height = extended.shape[0] - 2 * RAD
    across = extended.shape[1]
    block_width = 128
    block_count = across // block_width
    widened = jnp.pad(extended, ((0, 0), (RAD, RAD)))
    blocks = jnp.stack(
        [
            widened[:, start * block_width : start * block_width + block_width + 2 * RAD]
            for start in range(block_count)
        ]
    )
    col_table = jnp.transpose(band_table(profiles, block_width, block_width + 2 * RAD), (0, 2, 1))
    columns = jnp.einsum("srx,kxc->krsc", blocks, col_table, precision=lax.Precision.HIGHEST)
    columns = columns.reshape(NPROF, extended.shape[0], across)
    row_table = band_table(profiles, height, height + 2 * RAD)
    images = jnp.einsum("lhr,krc->klhc", row_table, columns, precision=lax.Precision.HIGHEST)
    return images.reshape(NPROF * NPROF, height, across)


def solve_kernel(normal_mat, normal_rhs):
    count = normal_mat.shape[0]
    factor = jnp.linalg.cholesky(normal_mat + ridge * jnp.eye(count, dtype=jnp.float32))
    return jax.scipy.linalg.cho_solve((factor, True), normal_rhs)


def finish_step(normal_mat, normal_rhs, flattened, usable, noise_var, image_sci):
    kernel_coef = jax.vmap(solve_kernel)(normal_mat, normal_rhs)
    fitted = jnp.einsum(
        "vb,bp->vp", kernel_coef, flattened, precision=lax.Precision.HIGHEST
    ).reshape(image_sci.shape)
    return usable * (image_sci - fitted) / jnp.sqrt(noise_var)


def shards(templates, owners, science, sci_var, bad_pixels):
    own_pair = templates[0]
    visit_count = science.shape[1]
    basis_count = NPROF * NPROF
    results = []
    for current in range(STEPS):
        owner_index = owners[current]
        arrived = from_root(own_pair, "visit", owner_index)
        extended = padded(arrived[0], (("patch", 0),), RAD)
        tile_var = arrived[1]
        images = basis_images(extended)
        flattened = images.reshape(basis_count, -1)
        usable = (1 - bad_pixels[current]).astype(jnp.float32)
        noise_var = sci_var[current] + tile_var[None]
        weight = usable / noise_var
        weighted = (images[None] * weight[:, None]).reshape(visit_count, basis_count, -1)
        normal_mat = jnp.einsum("vbp,cp->vbc", weighted, flattened, precision=lax.Precision.HIGHEST)
        normal_rhs = jnp.einsum(
            "cp,vp->vc",
            flattened,
            (weight * science[current]).reshape(visit_count, -1),
            precision=lax.Precision.HIGHEST,
        )
        summed_mat, summed_rhs = lax.psum((normal_mat, normal_rhs), "patch")
        results.append(
            finish_step(summed_mat, summed_rhs, flattened, usable, noise_var, science[current])
        )
    return jnp.stack(results)


def solution(mesh):
    return jax.shard_map(
        shards,
        mesh=mesh,
        in_specs=(
            P("visit", None, "patch", None),
            P(),
            P(None, "visit", "patch", None),
            P(None, "visit", "patch", None),
            P(None, "visit", "patch", None),
        ),
        out_specs=P(None, "visit", "patch", None),
        check_vma=False,
    )
```

profile of v0, /device:TPU:4, one launch (start us, length us, event | category | flops | bytes accessed | tf_op | source)
XLA Modules:
  0.0 429.1 jit_solution(2009927834076208268)
XLA Ops:
  6.8 1.4 fusion.136
  9.5 1.6 select_bitcast_fusion.1
  12.7 263.9 %all-reduce.6.cloned.1.call-done = (f32[2,16,1024]{2,1,0:T(8,128)}, f32[2,16,1024]{2,1,0:T(8,128)}) async-done(((f32[2,16,1024]{2,1,0:T(8,128)}, f32[2,16,1024]{2,1,0:T(8,128)}), (f32[2,16,1024]{2,1,0:T(8,128)}, f32[2,16,1024]{2,1,0:T(8,128)})) %all-reduce.6.cloned.1.call-update) | async-done | bytes 262160 | tf_op jit(solution)/shard_map/psum | solution.py:15
  277.5 1.9 collective-permute-start.2
  279.5 7.3 %collective-permute-start.3 = (f32[10,1024]{1,0:T(8,128)S(1)}, f32[10,1024]{1,0:T(8,128)S(1)}, u32[]{:S(2)}, u32[]{:S(2)}) collective-permute-start(f32[10,1024]{1,0:T(8,128)S(1)} %get-tuple-element.24), channel_id=1, source_target_pairs={{1,0},{2,1},{3,2},{4,3},{5,4},{6,5},{7,6},{8,7},{9,8},{10,9},{11,1... | collective-permute-start | bytes 122888 | tf_op jit(solution)/shard_map/ppermute | solution.py:28
  287.6 1.9 collective-permute-start
  289.6 7.3 %collective-permute-start.1 = (f32[10,1024]{1,0:T(8,128)S(1)}, f32[10,1024]{1,0:T(8,128)S(1)}, u32[]{:S(2)}, u32[]{:S(2)}) collective-permute-start(f32[10,1024]{1,0:T(8,128)S(1)} %get-tuple-element.22), channel_id=1, source_target_pairs={{1,0},{2,1},{3,2},{4,3},{5,4},{6,5},{7,6},{8,7},{9,8},{10,9},{11,1... | collective-permute-start | bytes 122888 | tf_op jit(solution)/shard_map/ppermute | solution.py:28
  296.9 1.0 fusion.59
  300.6 1.0 convolution_bitcast_fusion
  303.1 1.6 bitcast_multiply_fusion.1
  305.0 1.6 bitcast_multiply_fusion
  307.3 1.2 copy.27
  308.5 1.2 copy.28
  309.7 1.8 convolution_bitcast_fusion.3
  311.6 2.5 fusion.137
  314.4 1.2 copy.31
  315.6 1.2 copy.32
  316.8 2.4 convolution_bitcast_fusion.2
  319.3 2.3 fusion.138
  321.6 70.9 %all-reduce.3 = (f32[1,25,25]{1,2,0:T(8,128)}, f32[1,25]{1,0:T(1,128)}, f32[1,25,25]{1,2,0:T(8,128)}, f32[1,25]{1,0:T(1,128)}) all-reduce(f32[1,25,25]{1,2,0:T(8,128)} %convolution_bitcast_fusion.2, f32[1,25]{1,0:T(1,128)} %fusion.138, ...), channel_id=1, replica_groups=mesh['visit'=32,'patch'=16] {'patch'}, use_global_device_ids=true, to_apply=%region_6.9 | all-reduce | flops 1300 | bytes 10400 | tf_op jit(solution)/shard_map/psum | solution.py:116
  392.5 1.3 convert_add_fusion
  394.6 1.3 fusion.86
  396.0 3.0 custom-call.12
  399.6 1.2 fusion.83
  400.8 2.6 custom-call.13
  404.9 1.3 convert_add_fusion.1
  407.0 1.3 fusion.89
  408.3 3.0 custom-call.10
  412.1 1.2 fusion.82
  413.3 2.6 custom-call.11
  416.9 2.6 fusion
  419.5 2.0 fusion.2
  (132 shorter events, 14.8 us)
Async XLA Ops:
  6.5 5.0 %copy-start.8 = (f32[5]{0:T(128)S(1)}, f32[5]{0:T(128)}, u32[]{:S(2)}) copy-start(f32[5]{0:T(128)} %constant.163) | copy-start | bytes 64
  6.5 5.0 %copy-start.9 = (f32[5]{0:T(128)S(1)}, f32[5]{0:T(128)}, u32[]{:S(2)}) copy-start(f32[5]{0:T(128)} %constant.161) | copy-start | bytes 64
  6.5 5.0 %copy-start.10 = (f32[5]{0:T(128)S(1)}, f32[5]{0:T(128)}, u32[]{:S(2)}) copy-start(f32[5]{0:T(128)} %constant.159) | copy-start | bytes 64
  6.5 5.1 %copy-start.11 = (f32[5]{0:T(128)S(1)}, f32[5]{0:T(128)}, u32[]{:S(2)}) copy-start(f32[5]{0:T(128)} %constant.157) | copy-start | bytes 64
  6.5 5.1 %copy-start.12 = (f32[5]{0:T(128)S(1)}, f32[5]{0:T(128)}, u32[]{:S(2)}) copy-start(f32[5]{0:T(128)} %constant.155) | copy-start | bytes 64
  6.6 5.1 %copy-start.13 = (f32[5]{0:T(128)S(1)}, f32[5]{0:T(128)}, u32[]{:S(2)}) copy-start(f32[5]{0:T(128)} %constant.153) | copy-start | bytes 64
  6.6 5.1 %copy-start.14 = (f32[5]{0:T(128)S(1)}, f32[5]{0:T(128)}, u32[]{:S(2)}) copy-start(f32[5]{0:T(128)} %constant.151) | copy-start | bytes 64
  6.6 5.1 %copy-start.15 = (f32[5]{0:T(128)S(1)}, f32[5]{0:T(128)}, u32[]{:S(2)}) copy-start(f32[5]{0:T(128)} %constant.149) | copy-start | bytes 64
  6.6 5.1 %copy-start.16 = (f32[5]{0:T(128)S(1)}, f32[5]{0:T(128)}, u32[]{:S(2)}) copy-start(f32[5]{0:T(128)} %constant.147) | copy-start | bytes 64
  6.6 5.1 %copy-start.17 = (f32[5]{0:T(128)S(1)}, f32[5]{0:T(128)}, u32[]{:S(2)}) copy-start(f32[5]{0:T(128)} %constant.145) | copy-start | bytes 64
  6.6 5.1 %copy-start.18 = (f32[5]{0:T(128)S(1)}, f32[5]{0:T(128)}, u32[]{:S(2)}) copy-start(f32[5]{0:T(128)} %constant.143) | copy-start | bytes 64
  6.6 5.1 %copy-start.19 = (f32[5]{0:T(128)S(1)}, f32[5]{0:T(128)}, u32[]{:S(2)}) copy-start(f32[5]{0:T(128)} %constant.141) | copy-start | bytes 64
  6.6 5.0 %copy-start.20 = (f32[5]{0:T(128)S(1)}, f32[5]{0:T(128)}, u32[]{:S(2)}) copy-start(f32[5]{0:T(128)} %constant.139) | copy-start | bytes 64
  6.7 5.0 %copy-start.21 = (f32[5]{0:T(128)S(1)}, f32[5]{0:T(128)}, u32[]{:S(2)}) copy-start(f32[5]{0:T(128)} %constant.137) | copy-start | bytes 64
  6.7 5.0 %copy-start.22 = (f32[5]{0:T(128)S(1)}, f32[5]{0:T(128)}, u32[]{:S(2)}) copy-start(f32[5]{0:T(128)} %constant.135) | copy-start | bytes 64
  6.7 5.0 %copy-start.23 = (f32[5]{0:T(128)S(1)}, f32[5]{0:T(128)}, u32[]{:S(2)}) copy-start(f32[5]{0:T(128)} %constant.133) | copy-start | bytes 64
  6.7 5.0 %copy-start.24 = (f32[5]{0:T(128)S(1)}, f32[5]{0:T(128)}, u32[]{:S(2)}) copy-start(f32[5]{0:T(128)} %constant.131) | copy-start | bytes 64
  6.7 5.0 %copy-start.25 = (f32[5]{0:T(128)S(1)}, f32[5]{0:T(128)}, u32[]{:S(2)}) copy-start(f32[5]{0:T(128)} %constant.129) | copy-start | bytes 64
  6.7 5.0 %copy-start.26 = (f32[5]{0:T(128)S(1)}, f32[5]{0:T(128)}, u32[]{:S(2)}) copy-start(f32[5]{0:T(128)} %constant.127) | copy-start | bytes 64
  6.7 5.0 %copy-start.27 = (f32[5]{0:T(128)S(1)}, f32[5]{0:T(128)}, u32[]{:S(2)}) copy-start(f32[5]{0:T(128)} %constant.125) | copy-start | bytes 64
  6.7 5.0 %copy-start.28 = (f32[5]{0:T(128)S(1)}, f32[5]{0:T(128)}, u32[]{:S(2)}) copy-start(f32[5]{0:T(128)} %constant.123) | copy-start | bytes 64
  6.8 269.8 %all-reduce.6.cloned.1.call-start = ((), (), s32[]{:S(2)}) async-start(), calls=%async_computation | async-start | bytes 524288 | tf_op jit(solution)/shard_map/psum | solution.py:15
  11.3 285.5 %copy-start.2 = (f32[2,1,16,1024]{3,2,1,0:T(8,128)S(1)}, f32[2,1,16,1024]{3,2,1,0:T(8,128)}, u32[]{:S(2)}) copy-start(f32[2,1,16,1024]{3,2,1,0:T(8,128)} %param.12) | copy-start | bytes 393220
  11.3 285.5 %copy-start.3 = (f32[2,1,16,1024]{3,2,1,0:T(8,128)S(1)}, f32[2,1,16,1024]{3,2,1,0:T(8,128)}, u32[]{:S(2)}) copy-start(f32[2,1,16,1024]{3,2,1,0:T(8,128)} %param.13) | copy-start | bytes 393220
  11.3 285.5 %copy-start.4 = (s32[2,1,16,1024]{3,2,1,0:T(8,128)S(1)}, s32[2,1,16,1024]{3,2,1,0:T(8,128)}, u32[]{:S(2)}) copy-start(s32[2,1,16,1024]{3,2,1,0:T(8,128)} %param.14) | copy-start | bytes 393220
  277.5 21.7 %collective-permute-start.2 = (f32[10,1024]{1,0:T(8,128)S(1)}, f32[10,1024]{1,0:T(8,128)S(1)}, u32[]{:S(2)}, u32[]{:S(2)}) collective-permute-start(f32[10,1024]{1,0:T(8,128)S(1)} %get-tuple-element.23), channel_id=1, source_target_pairs={{0,1},{1,2},{2,3},{3,4},{4,5},{5,6},{6,7},{7,8},{8,9},{9,10},{10,1... | collective-permute-start | bytes 122888 | tf_op jit(solution)/shard_map/ppermute | solution.py:26
  279.5 19.8 %collective-permute-start.3 = (f32[10,1024]{1,0:T(8,128)S(1)}, f32[10,1024]{1,0:T(8,128)S(1)}, u32[]{:S(2)}, u32[]{:S(2)}) collective-permute-start(f32[10,1024]{1,0:T(8,128)S(1)} %get-tuple-element.24), channel_id=1, source_target_pairs={{1,0},{2,1},{3,2},{4,3},{5,4},{6,5},{7,6},{8,7},{9,8},{10,9},{11,1... | collective-permute-start | bytes 122888 | tf_op jit(solution)/shard_map/ppermute | solution.py:28
  287.6 11.6 %collective-permute-start = (f32[10,1024]{1,0:T(8,128)S(1)}, f32[10,1024]{1,0:T(8,128)S(1)}, u32[]{:S(2)}, u32[]{:S(2)}) collective-permute-start(f32[10,1024]{1,0:T(8,128)S(1)} %get-tuple-element.21), channel_id=1, source_target_pairs={{0,1},{1,2},{2,3},{3,4},{4,5},{5,6},{6,7},{7,8},{8,9},{9,10},{10,1... | collective-permute-start | bytes 122888 | tf_op jit(solution)/shard_map/ppermute | solution.py:26
  289.6 9.7 %collective-permute-start.1 = (f32[10,1024]{1,0:T(8,128)S(1)}, f32[10,1024]{1,0:T(8,128)S(1)}, u32[]{:S(2)}, u32[]{:S(2)}) collective-permute-start(f32[10,1024]{1,0:T(8,128)S(1)} %get-tuple-element.22), channel_id=1, source_target_pairs={{1,0},{2,1},{3,2},{4,3},{5,4},{6,5},{7,6},{8,7},{9,8},{10,9},{11,1... | collective-permute-start | bytes 122888 | tf_op jit(solution)/shard_map/ppermute | solution.py:28
  416.9 4.6 %copy-start = (f32[2,16,1024]{2,1,0:T(8,128)S(1)}, f32[2,16,1024]{2,1,0:T(8,128)}, u32[]{:S(2)}) copy-start(f32[2,16,1024]{2,1,0:T(8,128)} %get-tuple-element.6) | copy-start | bytes 393220
  416.9 4.6 %copy-start.1 = (f32[2,16,1024]{2,1,0:T(8,128)S(1)}, f32[2,16,1024]{2,1,0:T(8,128)}, u32[]{:S(2)}) copy-start(f32[2,16,1024]{2,1,0:T(8,128)} %get-tuple-element.8) | copy-start | bytes 393220
  416.9 4.6 %copy-start.5 = (s32[2,1,16,1024]{3,2,1,0:T(8,128)S(1)}, s32[2,1,16,1024]{3,2,1,0:T(8,128)}, u32[]{:S(2)}) copy-start(s32[2,1,16,1024]{3,2,1,0:T(8,128)} %param.14) | copy-start | bytes 393220
  (2 other events, 4.3 us)
Sparse Core Ops, SparseCore 0:
  11.2 265.3 all-reduce.5
where the time goes:
time: 430 us; the launch traced here: 429 us
  waiting for transfers between devices  264 us (61%)
  blocking collectives  70.9 us (16%)
  other arithmetic  24.9 us (6%)
  matrix products  21.2 us (5%)
  starting transfers between devices  18.4 us (4%)
  between operations  15.5 us (4%)
  local copies, waits for them, and re-layouts  14.3 us (3%)
    psum x1, waiting for transfers between devices, from_root(): return lax.psum(block, axis)  264 us
    psum x1, blocking collectives, shards(): summed_mat, summed_rhs = lax.psum((normal_mat, normal_rhs), 'patch')  70.9 us
    ppermute x2, starting transfers between devices, padded(): lax.ppermute(head, axis, [((i + 1) % count, i) for i in range(ends)])  14.5 us
  transfers between devices with their start and end apart: 5, of which 1 were waited for; matrix products, arithmetic and copies ran while one was open for 1% of the time, Pallas kernels for 0%

commit v1 on v0

--- a/solution.py
+++ b/solution.py
@@ -3,16 +3,18 @@
 import numpy as np
 from jax import lax
 from jax.sharding import PartitionSpec as P
+from jax.lax import all_gather
 
 NPROF = 5
 RAD = 10
 STEPS = 2
 ridge = 1.0
+rest_panels = lambda view, axis_key: all_gather(view, axis_key).sum(axis=0)
 
 
 def from_root(block, axis, holder):
     block = jnp.where(lax.axis_index(axis) == holder, block, jnp.zeros_like(block))
-    return lax.psum(block, axis)
+    return rest_panels(block, axis)
 
 
 def padded(cells, sides, width):

time: 430 us -> 447 us (1.040)
  waiting for transfers between devices: 264 us -> 272 us
  other arithmetic: 24.9 us -> 29.5 us
    all_gather x0 -> x2, waiting for transfers between devices: none -> 271 us  [rest_panels = lambda view, axis_key: all_gather(view, axis_key).sum(axis=0)]
    psum x1 -> x0, waiting for transfers between devices: 264 us -> none  [from_root(): return lax.psum(block, axis)]
    reduce_sum x0 -> x2, other arithmetic: none -> 4.86 us  [rest_panels = lambda view, axis_key: all_gather(view, axis_key).sum(axis=0)]
    unnamed x82 -> x86, local copies, waits for them, and re-layouts: 8.57 us -> 11.6 us
  transfers between devices with their start and end apart: 5 -> 6, of which waited for: 1 -> 2; matrix products, arithmetic and copies ran while one was open for 1% -> 2% of each run, Pallas kernels for 0% -> 0%
where the time goes in v1:
time: 447 us; the launch traced here: 445 us
  waiting for transfers between devices  272 us (61%)
  blocking collectives  71 us (16%)
  other arithmetic  29.5 us (7%)
  matrix products  23.2 us (5%)
  starting transfers between devices  18.7 us (4%)
  local copies, waits for them, and re-layouts  15.5 us (3%)
  between operations  15.5 us (3%)
    all_gather x2, waiting for transfers between devices, rest_panels = lambda view, axis_key: all_gather(view, axis_key).sum(axis=0)  271 us
    psum x1, blocking collectives, shards(): summed_mat, summed_rhs = lax.psum((normal_mat, normal_rhs), 'patch')  71 us
    ppermute x2, starting transfers between devices, padded(): lax.ppermute(head, axis, [((i + 1) % count, i) for i in range(ends)])  14.8 us
    unnamed x86, local copies, waits for them, and re-layouts  11.6 us
  transfers between devices with their start and end apart: 6, of which 2 were waited for; matrix products, arithmetic and copies ran while one was open for 2% of the time, Pallas kernels for 0%

profile of v1, /device:TPU:4, one launch (start us, length us, event | category | flops | bytes accessed | tf_op | source)
XLA Modules:
  0.0 445.2 jit_solution(17545082469773506719)
XLA Ops:
  6.8 1.4 fusion.136
  9.5 1.6 broadcast_select_fusion.1
  13.4 143.4 %all-gather.5.cloned.1.call-done = f32[32,2,16,1024]{3,2,1,0:T(8,128)} async-done(((f32[1,2,16,1024]{3,2,1,0:T(8,128)}), f32[32,2,16,1024]{3,2,1,0:T(8,128)}) %all-gather.5.cloned.1.call-update) | async-done | bytes 4194320 | tf_op jit(solution)/shard_map/all_gather | solution.py:12
  156.8 2.4 reduce_sum.19
  159.3 1.9 collective-permute-start.2
  161.2 7.4 %collective-permute-start.3 = (f32[10,1024]{1,0:T(8,128)S(1)}, f32[10,1024]{1,0:T(8,128)S(1)}, u32[]{:S(2)}, u32[]{:S(2)}) collective-permute-start(f32[10,1024]{1,0:T(8,128)S(1)} %get-tuple-element.24), channel_id=1, source_target_pairs={{1,0},{2,1},{3,2},{4,3},{5,4},{6,5},{7,6},{8,7},{9,8},{10,9},{11,1... | collective-permute-start | bytes 122888 | tf_op jit(solution)/shard_map/ppermute | solution.py:30
  168.6 127.5 %all-gather.3.cloned.1.call-done = f32[32,2,16,1024]{3,2,1,0:T(8,128)} async-done(((f32[1,2,16,1024]{3,2,1,0:T(8,128)}), f32[32,2,16,1024]{3,2,1,0:T(8,128)}) %all-gather.3.cloned.1.call-update) | async-done | bytes 4194320 | tf_op jit(solution)/shard_map/all_gather | solution.py:12
  296.2 2.4 reduce_sum.18
  298.6 1.9 collective-permute-start
  300.5 7.4 %collective-permute-start.1 = (f32[10,1024]{1,0:T(8,128)S(1)}, f32[10,1024]{1,0:T(8,128)S(1)}, u32[]{:S(2)}, u32[]{:S(2)}) collective-permute-start(f32[10,1024]{1,0:T(8,128)S(1)} %get-tuple-element.20), channel_id=1, source_target_pairs={{1,0},{2,1},{3,2},{4,3},{5,4},{6,5},{7,6},{8,7},{9,8},{10,9},{11,1... | collective-permute-start | bytes 122888 | tf_op jit(solution)/shard_map/ppermute | solution.py:30
  312.0 2.7 bitcast_multiply_fusion.1
  314.8 1.7 pad.18
  318.4 2.5 bitcast_multiply_fusion
  322.8 1.2 copy.33
  325.6 1.8 convolution_bitcast_fusion.3
  327.5 2.5 fusion.137
  330.3 1.2 copy.37
  332.7 2.4 convolution_bitcast_fusion.2
  335.2 2.2 fusion.138
  337.4 71.0 %all-reduce.2 = (f32[1,25,25]{1,2,0:T(8,128)}, f32[1,25]{1,0:T(1,128)}, f32[1,25,25]{1,2,0:T(8,128)}, f32[1,25]{1,0:T(1,128)}) all-reduce(f32[1,25,25]{1,2,0:T(8,128)} %convolution_bitcast_fusion.2, f32[1,25]{1,0:T(1,128)} %fusion.138, ...), channel_id=1, replica_groups=mesh['visit'=32,'patch'=16] {'patch'}, use_global_device_ids=true, to_apply=%region_6.9 | all-reduce | flops 1300 | bytes 10400 | tf_op jit(solution)/shard_map/psum | solution.py:118
  408.5 1.3 convert_add_fusion
  410.6 1.3 fusion.86
  411.9 3.0 custom-call.12
  415.6 1.2 fusion.83
  416.8 2.6 custom-call.13
  420.9 1.3 convert_add_fusion.1
  423.0 1.3 fusion.89
  424.4 3.0 custom-call.10
  428.1 1.2 fusion.82
  429.3 2.6 custom-call.11
  432.9 2.6 fusion
  435.6 2.0 fusion.2
  (141 shorter events, 19.2 us)
Async XLA Ops:
  6.5 5.8 %copy-start.10 = (f32[5]{0:T(128)S(1)}, f32[5]{0:T(128)}, u32[]{:S(2)}) copy-start(f32[5]{0:T(128)} %constant.164) | copy-start | bytes 64
  6.5 5.8 %copy-start.11 = (f32[5]{0:T(128)S(1)}, f32[5]{0:T(128)}, u32[]{:S(2)}) copy-start(f32[5]{0:T(128)} %constant.162) | copy-start | bytes 64
  6.5 5.8 %copy-start.12 = (f32[5]{0:T(128)S(1)}, f32[5]{0:T(128)}, u32[]{:S(2)}) copy-start(f32[5]{0:T(128)} %constant.160) | copy-start | bytes 64
  6.5 5.8 %copy-start.13 = (f32[5]{0:T(128)S(1)}, f32[5]{0:T(128)}, u32[]{:S(2)}) copy-start(f32[5]{0:T(128)} %constant.158) | copy-start | bytes 64
  6.5 5.8 %copy-start.14 = (f32[5]{0:T(128)S(1)}, f32[5]{0:T(128)}, u32[]{:S(2)}) copy-start(f32[5]{0:T(128)} %constant.156) | copy-start | bytes 64
  6.6 5.8 %copy-start.15 = (f32[5]{0:T(128)S(1)}, f32[5]{0:T(128)}, u32[]{:S(2)}) copy-start(f32[5]{0:T(128)} %constant.154) | copy-start | bytes 64
  6.6 5.8 %copy-start.16 = (f32[5]{0:T(128)S(1)}, f32[5]{0:T(128)}, u32[]{:S(2)}) copy-start(f32[5]{0:T(128)} %constant.152) | copy-start | bytes 64
  6.6 5.8 %copy-start.17 = (f32[5]{0:T(128)S(1)}, f32[5]{0:T(128)}, u32[]{:S(2)}) copy-start(f32[5]{0:T(128)} %constant.150) | copy-start | bytes 64
  6.6 5.8 %copy-start.18 = (f32[5]{0:T(128)S(1)}, f32[5]{0:T(128)}, u32[]{:S(2)}) copy-start(f32[5]{0:T(128)} %constant.148) | copy-start | bytes 64
  6.6 5.8 %copy-start.19 = (f32[5]{0:T(128)S(1)}, f32[5]{0:T(128)}, u32[]{:S(2)}) copy-start(f32[5]{0:T(128)} %constant.146) | copy-start | bytes 64
  6.6 5.8 %copy-start.20 = (f32[5]{0:T(128)S(1)}, f32[5]{0:T(128)}, u32[]{:S(2)}) copy-start(f32[5]{0:T(128)} %constant.144) | copy-start | bytes 64
  6.6 5.8 %copy-start.21 = (f32[5]{0:T(128)S(1)}, f32[5]{0:T(128)}, u32[]{:S(2)}) copy-start(f32[5]{0:T(128)} %constant.142) | copy-start | bytes 64
  6.6 5.8 %copy-start.22 = (f32[5]{0:T(128)S(1)}, f32[5]{0:T(128)}, u32[]{:S(2)}) copy-start(f32[5]{0:T(128)} %constant.140) | copy-start | bytes 64
  6.7 5.8 %copy-start.23 = (f32[5]{0:T(128)S(1)}, f32[5]{0:T(128)}, u32[]{:S(2)}) copy-start(f32[5]{0:T(128)} %constant.138) | copy-start | bytes 64
  6.7 5.8 %copy-start.24 = (f32[5]{0:T(128)S(1)}, f32[5]{0:T(128)}, u32[]{:S(2)}) copy-start(f32[5]{0:T(128)} %constant.136) | copy-start | bytes 64
  6.7 5.8 %copy-start.25 = (f32[5]{0:T(128)S(1)}, f32[5]{0:T(128)}, u32[]{:S(2)}) copy-start(f32[5]{0:T(128)} %constant.134) | copy-start | bytes 64
  6.7 5.8 %copy-start.26 = (f32[5]{0:T(128)S(1)}, f32[5]{0:T(128)}, u32[]{:S(2)}) copy-start(f32[5]{0:T(128)} %constant.132) | copy-start | bytes 64
  6.7 5.8 %copy-start.27 = (f32[5]{0:T(128)S(1)}, f32[5]{0:T(128)}, u32[]{:S(2)}) copy-start(f32[5]{0:T(128)} %constant.130) | copy-start | bytes 64
  6.7 5.8 %copy-start.28 = (f32[5]{0:T(128)S(1)}, f32[5]{0:T(128)}, u32[]{:S(2)}) copy-start(f32[5]{0:T(128)} %constant.128) | copy-start | bytes 64
  6.7 5.7 %copy-start.29 = (f32[5]{0:T(128)S(1)}, f32[5]{0:T(128)}, u32[]{:S(2)}) copy-start(f32[5]{0:T(128)} %constant.126) | copy-start | bytes 64
  6.7 5.7 %copy-start.30 = (f32[5]{0:T(128)S(1)}, f32[5]{0:T(128)}, u32[]{:S(2)}) copy-start(f32[5]{0:T(128)} %constant.124) | copy-start | bytes 64
  6.8 150.1 %all-gather.5.cloned.1.call-start = ((), (), s32[]{:S(2)}) async-start(), calls=%async_computation.1 | async-start | bytes 4325376 | tf_op jit(solution)/shard_map/all_gather | solution.py:12
  11.1 285.0 %all-gather.3.cloned.1.call-start = ((), (), s32[]{:S(2)}) async-start(), calls=%async_computation | async-start | bytes 4325376 | tf_op jit(solution)/shard_map/all_gather | solution.py:12
  159.3 150.8 %collective-permute-start.2 = (f32[10,1024]{1,0:T(8,128)S(1)}, f32[10,1024]{1,0:T(8,128)S(1)}, u32[]{:S(2)}, u32[]{:S(2)}) collective-permute-start(f32[10,1024]{1,0:T(8,128)S(1)} %get-tuple-element.23), channel_id=1, source_target_pairs={{0,1},{1,2},{2,3},{3,4},{4,5},{5,6},{6,7},{7,8},{8,9},{9,10},{10,1... | collective-permute-start | bytes 122888 | tf_op jit(solution)/shard_map/ppermute | solution.py:28
  161.2 146.8 %copy-start.2 = (f32[2,1,16,1024]{3,2,1,0:T(8,128)S(1)}, f32[2,1,16,1024]{3,2,1,0:T(8,128)}, u32[]{:S(2)}) copy-start(f32[2,1,16,1024]{3,2,1,0:T(8,128)} %param.12) | copy-start | bytes 393220
  161.2 146.8 %copy-start.4 = (f32[2,1,16,1024]{3,2,1,0:T(8,128)S(1)}, f32[2,1,16,1024]{3,2,1,0:T(8,128)}, u32[]{:S(2)}) copy-start(f32[2,1,16,1024]{3,2,1,0:T(8,128)} %param.13) | copy-start | bytes 393220
  161.2 146.8 %copy-start.6 = (s32[2,1,16,1024]{3,2,1,0:T(8,128)S(1)}, s32[2,1,16,1024]{3,2,1,0:T(8,128)}, u32[]{:S(2)}) copy-start(s32[2,1,16,1024]{3,2,1,0:T(8,128)} %param.14) | copy-start | bytes 393220
  161.2 148.9 %collective-permute-start.3 = (f32[10,1024]{1,0:T(8,128)S(1)}, f32[10,1024]{1,0:T(8,128)S(1)}, u32[]{:S(2)}, u32[]{:S(2)}) collective-permute-start(f32[10,1024]{1,0:T(8,128)S(1)} %get-tuple-element.24), channel_id=1, source_target_pairs={{1,0},{2,1},{3,2},{4,3},{5,4},{6,5},{7,6},{8,7},{9,8},{10,9},{11,1... | collective-permute-start | bytes 122888 | tf_op jit(solution)/shard_map/ppermute | solution.py:30
  298.6 11.5 %collective-permute-start = (f32[10,1024]{1,0:T(8,128)S(1)}, f32[10,1024]{1,0:T(8,128)S(1)}, u32[]{:S(2)}, u32[]{:S(2)}) collective-permute-start(f32[10,1024]{1,0:T(8,128)S(1)} %get-tuple-element.19), channel_id=1, source_target_pairs={{0,1},{1,2},{2,3},{3,4},{4,5},{5,6},{6,7},{7,8},{8,9},{9,10},{10,1... | collective-permute-start | bytes 122888 | tf_op jit(solution)/shard_map/ppermute | solution.py:28
  300.5 9.6 %collective-permute-start.1 = (f32[10,1024]{1,0:T(8,128)S(1)}, f32[10,1024]{1,0:T(8,128)S(1)}, u32[]{:S(2)}, u32[]{:S(2)}) collective-permute-start(f32[10,1024]{1,0:T(8,128)S(1)} %get-tuple-element.20), channel_id=1, source_target_pairs={{1,0},{2,1},{3,2},{4,3},{5,4},{6,5},{7,6},{8,7},{9,8},{10,9},{11,1... | collective-permute-start | bytes 122888 | tf_op jit(solution)/shard_map/ppermute | solution.py:30
  432.9 4.7 %copy-start.5 = (f32[2,1,16,1024]{3,2,1,0:T(8,128)S(1)}, f32[2,1,16,1024]{3,2,1,0:T(8,128)}, u32[]{:S(2)}) copy-start(f32[2,1,16,1024]{3,2,1,0:T(8,128)} %param.13) | copy-start | bytes 393220
  432.9 4.7 %copy-start.7 = (s32[2,1,16,1024]{3,2,1,0:T(8,128)S(1)}, s32[2,1,16,1024]{3,2,1,0:T(8,128)}, u32[]{:S(2)}) copy-start(s32[2,1,16,1024]{3,2,1,0:T(8,128)} %param.14) | copy-start | bytes 393220
  (5 other events, 12.0 us)
Sparse Core Ops, SparseCore 0:
  11.2 145.5 all-gather.4
  158.9 137.2 all-gather.2
